TPU v7x, 32 devices: a whole 2x2x4 slice. The times are simulated.
32 devices in a mesh: dp: 2 (over x), seq: 16 (over z, y, core).
Axes of the slice: x: 2, y: 2, z: 4, core: 2. Of those that a mesh axis runs over, the one named last changes fastest.
Arguments:
- queries: bfloat16 [2, 2048, 2048], P('dp', 'seq'), may hold values from -6 to 6
- keys: bfloat16 [2, 2048, 2048], P('dp', 'seq'), may hold values from -0.75 to 0.75
- values: bfloat16 [2, 2048, 2048], P('dp', 'seq'), may hold values from -6 to 6
- log_decay: float32 [2, 32, 2048], P('dp', None, 'seq'), may hold values from -0.7 to 0
- gain: float32 [2048], replicated, may hold values from 0.25 to 1.75
- d_out: bfloat16 [2, 2048, 2048], P('dp', 'seq'), may hold values from -12 to 12
Outputs:
- d_queries: bfloat16 [2, 2048, 2048], P('dp', 'seq')
- d_keys: bfloat16 [2, 2048, 2048], P('dp', 'seq')
- d_values: bfloat16 [2, 2048, 2048], P('dp', 'seq')
- d_log_decay: float32 [2, 32, 2048], P('dp', None, 'seq')
- d_gain: float32 [2048], replicated
All inputs are finite; a program needn't handle non-finite values.
Results may differ from a plain program's by a relative error of at most 0.001.
Values sent between devices are 32-bit elements; how exact they have to be, the bound alone decides.
A program may use at most 192 MiB of HBM per device.

v0:
```python
import functools

import jax
import jax.numpy as jnp
from jax import lax
from jax.experimental import pallas as pl
from jax.experimental.pallas import tpu as pltpu
from jax.sharding import PartitionSpec as P

EPSILON = 1e-06
HIGH = lax.Precision.HIGHEST
F32 = jnp.float32
BF16 = jnp.bfloat16
UNROLL = 2
WIDE = 4
VMEM = 58 * 1024 * 1024


def dot(a, b, contract, precision=None):
    return lax.dot_general(
        a, b, (contract, ((), ())), precision=precision, preferred_element_type=F32
    )


def nn(a, b, precision=None):
    return dot(a, b, ((1,), (0,)), precision)


def nt(a, b, precision=None):
    return dot(a, b, ((1,), (1,)), precision)


def tn(a, b):
    return dot(a, b, ((0,), (0,)))


def split(x):
    high = x.astype(BF16)
    return high, (x - high.astype(F32)).astype(BF16)


def rows(*parts):
    return jnp.concatenate(parts, axis=0)


def lanes(*parts):
    return jnp.concatenate(parts, axis=1)


def kernel(
    size,
    width,
    inputs,
    outputs,
    scratch,
):
    s = scratch
    dq_ref, dk_ref, dv_ref, dlog_ref, dgain_ref = s.dq, s.dk, s.dv, s.dlog, s.dgain
    q_ref, k_ref, v_ref, log_ref, gain_ref, do_ref = places = (
        s.q, s.k, s.v, s.log, s.gain, s.do
    )
    loads = [
        pltpu.make_async_copy(source, target, s.load.at[index])
        for index, (source, target) in enumerate(zip(inputs, places))
    ]
    q_load, k_load, v_load, log_load, gain_load, do_load = loads
    for load in (log_load, k_load, v_load, q_load, do_load, gain_load):
        load.start()
    seq_size, dp_size, levels = size
    length = q_ref.shape[0]
    pair_width = 2 * width
    pairs = q_ref.shape[1] // pair_width
    heads = 2 * pairs
    group = 2 ** levels
    chain = seq_size // group
    me = lax.axis_index("seq")
    dp = lax.axis_index("dp")

    def at_seq(index):
        return {"seq": index}

    def bit_of(value, level):
        return lax.rem(lax.div(value, 2 ** level), 2)

    def flipped(value, level):
        return value + 2 ** level * (1 - 2 * bit_of(value, level))

    place = lax.div(me, group)
    after = lax.rem(me + group, seq_size)
    before = lax.rem(me + seq_size - group, seq_size)
    seq_bits = seq_size.bit_length() - 1
    dp_bits = dp_size.bit_length() - 1
    partners = [at_seq(flipped(me, level)) for level in range(seq_bits)]
    partners += [{"dp": flipped(dp, level)} for level in range(dp_bits)]
    greeted = partners + [at_seq(after), at_seq(before)]

    barrier = pltpu.get_barrier_semaphore()
    for other in greeted:
        pl.semaphore_signal(
            barrier, inc=1, device_id=other, device_id_type=pl.DeviceIdType.MESH
        )

    def copy_to(source, target, send, recv, device):
        return pltpu.make_async_remote_copy(
            src_ref=source, dst_ref=target, send_sem=send, recv_sem=recv,
            device_id=device, device_id_type=pl.DeviceIdType.MESH,
        )

    lane_row = lax.broadcasted_iota(jnp.int32, (1, pair_width), 1)
    low_row = lane_row < width

    def low(shape):
        return lax.broadcasted_iota(jnp.int32, shape, 1) < width

    low_tok = low((length, pair_width))
    low_state = low((width, pair_width))

    def columns(pair):
        if isinstance(pair, int):
            return pl.ds(pair * pair_width, pair_width)
        return pl.ds(pl.multiple_of(pair * pair_width, pair_width), pair_width)

    def stacked(block):
        zero = jnp.zeros_like(block)
        return rows(jnp.where(low_tok, block, zero), jnp.where(low_tok, zero, block))

    def diagonal(state):
        zero = jnp.zeros_like(state)
        return rows(jnp.where(low_state, state, zero), jnp.where(low_state, zero, state))

    def packed(square):
        return jnp.where(low_state, square[:width], square[width:])

    upper_sub = lax.broadcasted_iota(jnp.int32, (pair_width, length), 0) < width

    def picked(broad):
        return jnp.where(upper_sub, broad[:, :length], broad[:, length:])

    def each(start, count, compute, unroll=UNROLL):
        if isinstance(count, int) and count % unroll:
            unroll = 1

        def body(index, carry):
            stores = []
            for offset in range(unroll):
                stores += compute(start + index * unroll + offset)
            for ref, where, value in stores:
                ref[where] = value
            return carry

        trips = count // unroll if isinstance(count, int) else lax.div(count, unroll)
        lax.fori_loop(0, trips, body, 0)

    ones_from = lax.broadcasted_iota(jnp.int32, (length, length), 0)
    ones_to = lax.broadcasted_iota(jnp.int32, (length, length), 1)
    causal = ones_from >= ones_to
    log_load.wait()
    log_block = log_ref[...]
    cum_rows = nn(log_block, (ones_from <= ones_to).astype(F32), HIGH)
    s.cum[...] = cum_rows
    s.late_rows[...] = jnp.exp(cum_rows[:, length - 1:length] - cum_rows)
    cum_columns = nt(causal.astype(F32), log_block, HIGH)

    k_load.wait()
    v_load.wait()
    for pair in range(pairs):
        first = jnp.broadcast_to(cum_columns[:, 2 * pair:2 * pair + 1], (length, length))
        second = jnp.broadcast_to(cum_columns[:, 2 * pair + 1:2 * pair + 2], (length, length))
        s.spread[2 * pair] = first
        s.spread[2 * pair + 1] = second
        mixed = jnp.where(low_tok, first, second)
        total = mixed[length - 1:length, :]
        s.grow[pair] = jnp.exp(mixed)
        late = jnp.exp(total - mixed)
        s.late[pair] = late
        s.decay[0, pair:pair + 1, :] = jnp.exp(total)

    def state_of(pair):
        key = k_ref[:, columns(pair)]
        high, rest = split(v_ref[:, columns(pair)].astype(F32) * s.late[pair])
        key_t = jnp.transpose(key)
        fresh = packed(nn(lanes(key_t, key_t), rows(high, rest)))
        return [(s.key_t, pair, key_t), (s.fresh, pair, fresh)]

    pl.semaphore_wait(barrier, len(greeted))

    bits = [bit_of(me, level) for level in range(levels)]
    halves = [pairs >> (level + 1) for level in range(levels)]
    keeps = [bit * half for bit, half in zip(bits, halves)]
    gives = [(1 - bit) * half for bit, half in zip(bits, halves)]
    bases = [0]
    for keep in keeps:
        bases.append(bases[-1] + keep)
    state_shape = (width, pair_width)

    def pieces(level):
        half = halves[level]
        if level == levels - 1:
            return [(i, 1) for i in range(half)]
        return [(gives[level + 1], half // 2), (keeps[level + 1], half // 2)]

    def scan(name, source, result, backward, produce, works, consume):
        x = s.scans[name]
        first_bit = 1 if backward else 0
        owned = [source] + [x.total[level] for level in range(levels)]
        outs = [result] + [x.prefix[level] for level in range(1, levels)]
        mine_first = [jnp.broadcast_to(bit, state_shape) == first_bit for bit in bits]
        row_first = [jnp.broadcast_to(bit, (1, pair_width)) == first_bit for bit in bits]
        partner = [at_seq(flipped(me, level)) for level in range(levels)]

        def up(level, index):
            offset, size = pieces(level)[index]
            return copy_to(
                owned[level].at[pl.ds(gives[level] + offset, size)],
                x.received[level].at[pl.ds(offset, size)],
                x.up_send.at[level, index], x.up_recv.at[level, index], partner[level],
            )

        def decay_copy(level):
            return copy_to(
                s.decay.at[level], s.decay_other.at[level],
                s.decay_send.at[level], s.decay_recv.at[level], partner[level],
            )

        def start_up(level):
            if not backward:
                decay_copy(level).start()
            for index in range(len(pieces(level))):
                up(level, index).start()

        def join(level, index):
            up(level, index).wait_recv()
            offset, size = pieces(level)[index]
            for i in range(size):
                own = owned[level][keeps[level] + offset + i]
                other = x.received[level][offset + i]
                row = pl.ds(bases[level] + keeps[level] + offset + i, 1)
                later_decay = jnp.where(
                    row_first[level], s.decay_other[level, row, :], s.decay[level, row, :]
                )
                earlier = jnp.where(mine_first[level], own, other)
                later = jnp.where(mine_first[level], other, own)
                x.first[level][offset + i] = earlier
                x.total[level][offset + i] = later_decay * earlier + later

        produce(gives[0], halves[0])
        start_up(0)
        produce(keeps[0], halves[0])
        for level in range(levels):
            works[level]()
            if not backward:
                decay_copy(level).wait()
                s.decay[level + 1] = s.decay[level] * s.decay_other[level]
            if level < levels - 1:
                join(level, 0)
                start_up(level + 1)
                join(level, 1)

        start_place = chain - 1 if backward else 0
        stop_place = 0 if backward else chain - 1
        target = at_seq(before if backward else after)
        count = halves[-1]

        def link(i):
            return copy_to(
                x.chain_out.at[i], x.chain_in.at[i],
                x.chain_send.at[i], x.chain_recv.at[i], target,
            )

        def down(level, i):
            place_of = keeps[level] + i
            return copy_to(
                x.give[level].at[i], outs[level].at[place_of],
                x.down_send.at[level, i], x.down_recv.at[level, i], partner[level],
            )

        def arrival(level, i):
            return copy_to(
                x.give[level].at[i], outs[level].at[gives[level] + i],
                x.down_send.at[level, i], x.down_recv.at[level, i], partner[level],
            )

        def descend(level, i, given):
            row = pl.ds(bases[level] + keeps[level] + i, 1)
            first_decay = jnp.where(
                row_first[level], s.decay[level, row, :], s.decay_other[level, row, :]
            )
            moved = first_decay * given + x.first[level][i]
            x.give[level][i] = jnp.where(mine_first[level], moved, given)
            down(level, i).start()
            own = jnp.where(mine_first[level], given, moved)
            outs[level][keeps[level] + i] = own
            if level > 0:
                descend(level - 1, keeps[level] + i, own)

        @pl.when(place == start_place)
        def _():
            x.chain_in[...] = jnp.zeros_like(x.chain_in)

        begins = (place == start_place).astype(jnp.int32)
        for i in range(count):
            join(levels - 1, i)
        works[levels](1 - begins)
        for i in range(count):
            @pl.when(place != start_place)
            def _(i=i):
                link(i).wait_recv()

            @pl.when(place != stop_place)
            def _(i=i):
                row = pl.ds(bases[levels] + i, 1)
                x.chain_out[i] = s.decay[levels, row, :] * x.chain_in[i] + owned[levels][i]
                link(i).start()

            descend(levels - 1, i, x.chain_in[i])
        works[levels + 1](begins)
        for level in range(levels - 1, 0, -1):
            order = range(halves[level])
            for i in order if level == levels - 1 else ordered(level):
                arrival(level, i).wait_recv()
                descend(level - 1, gives[level] + i, outs[level][gives[level] + i])
        consume(keeps[0], halves[0])
        for i in range(halves[0]):
            arrival(0, i).wait_recv()
        consume(gives[0], halves[0])

        for level in range(levels):
            for index in range(len(pieces(level))):
                up(level, index).wait_send()
            for i in range(halves[level]):
                down(level, i).wait_send()

        @pl.when(place != stop_place)
        def _():
            for i in range(count):
                link(i).wait_send()

    def ordered(level):
        half = halves[level + 1]
        return [keeps[level + 1] + i for i in range(half)] + [
            gives[level + 1] + i for i in range(half)
        ]

    def inside(pair):
        query = q_ref[:, columns(pair)]
        scores = nt(query, stacked(k_ref[:, columns(pair)]))
        tables = []
        for head in range(2):
            gap = s.spread[2 * pair + head] - s.cum[pl.ds(2 * pair + head, 1), :]
            tables.append(jnp.where(causal, jnp.exp(jnp.minimum(gap, 0.0)), 0.0))
        table = lanes(*tables)
        high, rest = split(scores * table)
        values = stacked(v_ref[:, columns(pair)])
        part = nn(lanes(high, rest), rows(values, values))
        return [
            (s.table, pair, table), (s.score_high, pair, high),
            (s.score_rest, pair, rest), (s.attended, pair, part),
            (s.query_t, pair, jnp.transpose(query)),
        ]

    def cut(compute):
        share = max(2, pairs // (2 * levels) // 2 * 2)
        counts = [2] + [share] * (levels - 1)
        left = pairs - sum(counts)
        middle = left // 2 // 2 * 2
        works, start = [], 0
        for count in counts:
            works.append(functools.partial(each, start, count, compute))
            start += count

        def waiting(flag):
            each(start, middle * flag, compute)

        def closing(flag):
            done = middle * (1 - flag)
            each(start + done, left - done, compute)

        return works + [waiting, closing]

    s.squares[...] = jnp.zeros_like(s.squares)
    s.products[...] = jnp.zeros_like(s.products)

    def attend(pair):
        query = q_ref[:, columns(pair)]
        high, rest = split(diagonal(s.start[pair]))
        carried = nn(lanes(query, query), rows(high, rest))
        attended = s.attended[pair] + s.grow[pair] * carried
        slope = do_ref[:, columns(pair)].astype(F32) * gain_ref[pl.ds(pair, 1), :]
        return attended, slope

    def attend_range(start, count):
        def body(index, carry):
            squares, products = s.squares[...], s.products[...]
            results = [attend(start + index * WIDE + offset) for offset in range(WIDE)]
            for offset, (attended, slope) in enumerate(results):
                s.attended[start + index * WIDE + offset] = attended
                squares = squares + attended * attended
                products = products + attended * slope
            s.squares[...] = squares
            s.products[...] = products
            return carry

        lax.fori_loop(0, count // WIDE, body, 0)

    q_load.wait()
    arrived = []

    def attend_after_loads(start, count):
        if not arrived:
            gain_load.wait()
            do_load.wait()
            arrived.append(True)
        attend_range(start, count)

    scan(
        "forward", s.fresh, s.start, False,
        lambda start, count: each(start, count, state_of, WIDE),
        cut(inside), attend_after_loads,
    )
    features = pairs * pair_width
    mean = jnp.sum(s.squares[...], axis=1, keepdims=True) / features
    inverse = 1.0 / jnp.sqrt(mean + EPSILON)
    weight = jnp.sum(s.products[...], axis=1, keepdims=True) / features * inverse * inverse * inverse
    s.inverse[...] = jnp.broadcast_to(inverse, (length, pair_width))
    s.weight[...] = jnp.broadcast_to(weight, (length, pair_width))

    def slopes(pair):
        cotangent = do_ref[:, columns(pair)].astype(F32)
        attended = s.attended[pair]
        inverse = s.inverse[...]
        gained = jnp.sum(attended * inverse * cotangent, axis=0, keepdims=True)
        slope = cotangent * gain_ref[pl.ds(pair, 1), :] * inverse - attended * s.weight[...]
        high, rest = split(slope)
        grown_high, grown_rest = split(slope * s.grow[pair])
        query_t = s.query_t[pair]
        incoming = packed(nn(lanes(query_t, query_t), rows(grown_high, grown_rest)))
        return [
            (s.slope_high, pair, high), (s.slope_rest, pair, rest),
            (s.incoming, pair, incoming),
            (s.gained, (0, pl.ds(pair, 1), slice(None)), gained),
        ]

    def gain_step(step):
        copy = copy_to(
            s.gained.at[step], s.gained_other.at[step],
            s.gain_send.at[step], s.gain_recv.at[step], partners[step],
        )
        return copy

    def gain_advance(step):
        gain_step(step).wait()
        s.gained[step + 1] = s.gained[step] + s.gained_other[step]
        if step + 1 < len(partners):
            gain_step(step + 1).start()

    def grads(pair):
        query, key = q_ref[:, columns(pair)], k_ref[:, columns(pair)]
        keys, values = stacked(key), stacked(v_ref[:, columns(pair)])
        high, rest = s.slope_high[pair], s.slope_rest[pair]
        from_values = nt(lanes(high, rest), lanes(values, values))
        inner_high, inner_rest = split(from_values * s.table[pair])
        state_high, state_rest = split(diagonal(s.start[pair]))
        carried = nt(lanes(high, rest, high), lanes(state_high, state_high, state_rest))
        d_query = nn(lanes(inner_high, inner_rest), rows(keys, keys)) + s.grow[pair] * carried
        query_t = s.query_t[pair]
        d_key_t = picked(nn(lanes(query_t, query_t), rows(inner_high, inner_rest)))
        score_high, score_rest = s.score_high[pair], s.score_rest[pair]
        high_t, rest_t = jnp.transpose(high), jnp.transpose(rest)
        d_value_t = picked(
            nn(lanes(high_t, high_t, rest_t), rows(score_high, score_rest, score_high))
        )
        change_high, change_rest = split(d_query * query.astype(F32))
        per_head = nt(lanes(sides, sides), lanes(change_high, change_rest))
        return [
            (dq_ref, (slice(None), columns(pair)), d_query.astype(BF16)),
            (s.query_rows, pair, per_head),
            (s.d_key_t, pair, d_key_t), (s.d_value, pair, jnp.transpose(d_value_t)),
        ]

    side_row = lax.broadcasted_iota(jnp.int32, (8, pair_width), 0)
    side_lane = lax.broadcasted_iota(jnp.int32, (8, pair_width), 1)
    sides = (side_row == (side_lane >= width).astype(jnp.int32)).astype(F32).astype(BF16)
    steps = len(partners)

    def with_gain(work, first, last):
        def run(*flag):
            work(*flag)
            for step in range(first, last):
                gain_advance(step)
        return run

    works = cut(grads)
    begun = []

    def produce_slopes(start, count):
        each(start, count, slopes, WIDE)
        begun.append(True)
        if len(begun) == 2:
            gain_step(0).start()

    spread_steps = [steps * i // (levels + 2) for i in range(levels + 3)]
    works = [
        with_gain(work, spread_steps[i], spread_steps[i + 1]) for i, work in enumerate(works)
    ]

    def store(index):
        return pltpu.make_async_copy(results[index], outputs[index], s.store.at[index, 0])

    results = (dq_ref, dk_ref, dv_ref, dlog_ref, dgain_ref)
    stores = []

    s.d_cum[...] = jnp.zeros_like(s.d_cum)
    s.ended[...] = jnp.zeros_like(s.ended)
    head_of = lax.broadcasted_iota(jnp.int32, (heads, pair_width), 0)
    side_of = (lax.broadcasted_iota(jnp.int32, (heads, pair_width), 1) >= width).astype(jnp.int32)

    def finish(pair):
        key, value = k_ref[:, columns(pair)], v_ref[:, columns(pair)]
        end = s.end[pair]
        high, rest = split(diagonal(end))
        late_t = jnp.where(
            upper_sub, s.late_rows[pl.ds(2 * pair, 1), :], s.late_rows[pl.ds(2 * pair + 1, 1), :]
        )
        d_key_t = s.d_key_t[pair] + late_t * nt(lanes(high, rest), lanes(value, value))
        d_value = s.d_value[pair] + s.late[pair] * nn(lanes(key, key), rows(high, rest))
        change = d_key_t * s.key_t[pair].astype(F32)
        first = s.query_rows[pair, 0:1] - jnp.sum(change[:width], axis=0, keepdims=True)
        second = s.query_rows[pair, 1:2] - jnp.sum(change[width:], axis=0, keepdims=True)
        d_cum = jnp.where(head_of == 2 * pair, first, 0.0)
        d_cum = jnp.where(head_of == 2 * pair + 1, second, d_cum)
        last_state = s.decay[0, pl.ds(pair, 1), :] * s.start[pair] + s.fresh[pair]
        ended = jnp.sum(last_state * end, axis=0, keepdims=True)
        ended = jnp.where(head_of == 2 * pair + side_of, ended, 0.0)
        return jnp.transpose(d_key_t.astype(BF16)), d_value.astype(BF16), d_cum, ended

    def finish_range(start, count):
        if not stores:
            dgain_ref[...] = s.gained[steps]
            begin = [store(0), store(4)]
            for copy in begin:
                copy.start()
            stores.extend(begin)

        def body(index, carry):
            total, ends = s.d_cum[...], s.ended[...]
            results = [finish(start + index * WIDE + offset) for offset in range(WIDE)]
            for offset, (d_key, d_value, d_cum, ended) in enumerate(results):
                pair = start + index * WIDE + offset
                dk_ref[:, columns(pair)] = d_key
                dv_ref[:, columns(pair)] = d_value
                total = total + d_cum
                ends = ends + ended
            s.d_cum[...] = total
            s.ended[...] = ends
            return carry

        lax.fori_loop(0, count // WIDE, body, 0)
        where = pl.ds(pl.multiple_of(start * pair_width, pair_width), count * pair_width)
        slot = len(stores) // 4
        for index in (1, 2):
            copy = pltpu.make_async_copy(
                results[index].at[:, where], outputs[index].at[:, where], s.store.at[index, slot]
            )
            copy.start()
            stores.append(copy)

    scan("backward", s.incoming, s.end, True, produce_slopes, works, finish_range)
    through = jnp.sum(s.ended[...], axis=1, keepdims=True)
    dlog_ref[...] = nn(s.d_cum[...], causal.astype(F32), HIGH) + through
    stores.append(store(3))
    stores[-1].start()
    for copy in stores:
        copy.wait()


def deliver(*refs):
    sources, targets, held, (read, wrote) = refs[:5], refs[5:10], refs[10:15], refs[15:]
    reads = [
        pltpu.make_async_copy(source, place, read.at[index])
        for index, (source, place) in enumerate(zip(sources, held))
    ]
    writes = [
        pltpu.make_async_copy(place, target, wrote.at[index])
        for index, (place, target) in enumerate(zip(held, targets))
    ]
    for copy in reads:
        copy.start()
    for copy, following in zip(reads, writes):
        copy.wait()
        following.start()
    for copy in writes:
        copy.wait()


class Bag:
    pass


def layout(length, pairs, width, levels, chained, steps):
    pair_width = 2 * width
    state = (width, pair_width)
    token = (length, pair_width)
    wide = (length, 2 * length)
    dma = pltpu.SemaphoreType.DMA

    def vmem(shape, dtype=F32):
        return pltpu.VMEM(shape, dtype)

    spec = {
        "cum": vmem((2 * pairs, length)),
        "spread": vmem((2 * pairs, length, length)),
        "grow": vmem((pairs,) + token),
        "late": vmem((pairs,) + token),
        "decay": vmem((levels + 1, pairs, pair_width)),
        "decay_other": vmem((levels, pairs, pair_width)),
        "decay_send": dma((levels,)),
        "decay_recv": dma((levels,)),
        "fresh": vmem((pairs,) + state),
        "start": vmem((pairs,) + state),
        "incoming": vmem((pairs,) + state),
        "end": vmem((pairs,) + state),
        "table": vmem((pairs,) + wide),
        "score_high": vmem((pairs,) + wide, BF16),
        "score_rest": vmem((pairs,) + wide, BF16),
        "attended": vmem((pairs,) + token),
        "squares": vmem(token),
        "products": vmem(token),
        "inverse": vmem(token),
        "weight": vmem(token),
        "slope_high": vmem((pairs,) + token, BF16),
        "slope_rest": vmem((pairs,) + token, BF16),
        "gained": vmem((steps + 1, pairs, pair_width)),
        "gained_other": vmem((steps, pairs, pair_width)),
        "gain_send": dma((steps,)),
        "gain_recv": dma((steps,)),
        "query_rows": vmem((pairs, 8, length)),
        "query_t": vmem((pairs, pair_width, length), BF16),
        "key_t": vmem((pairs, pair_width, length), BF16),
        "late_rows": vmem((2 * pairs, length)),
        "d_key_t": vmem((pairs, pair_width, length)),
        "ended": vmem((2 * pairs, pair_width)),
        "q": vmem((length, pairs * pair_width), BF16),
        "k": vmem((length, pairs * pair_width), BF16),
        "v": vmem((length, pairs * pair_width), BF16),
        "do": vmem((length, pairs * pair_width), BF16),
        "log": vmem((2 * pairs, length)),
        "gain": vmem((pairs, pair_width)),
        "load": dma((6,)),
        "store": dma((5, 2)),
        "dq": vmem((length, pairs * pair_width), BF16),
        "dk": vmem((length, pairs * pair_width), BF16),
        "dv": vmem((length, pairs * pair_width), BF16),
        "dlog": vmem((2 * pairs, length)),
        "dgain": vmem((pairs, pair_width)),
        "d_value": vmem((pairs,) + token),
        "d_cum": vmem((2 * pairs, length)),
    }
    kept = [pairs >> (level + 1) for level in range(levels)]
    for name in ("forward", "backward"):
        for level in range(levels):
            for part in ("received", "first", "total", "give"):
                spec[name, part, level] = vmem((kept[level],) + state)
            if level > 0:
                spec[name, "prefix", level] = vmem((kept[level - 1],) + state)
        spec[name, "chain_in"] = vmem((chained,) + state)
        spec[name, "chain_out"] = vmem((chained,) + state)
        for part in ("chain_send", "chain_recv"):
            spec[name, part] = dma((chained,))
        for part in ("up_send", "up_recv", "down_send", "down_recv"):
            spec[name, part] = dma((levels, pairs // 2))
    return spec


def gathered(keys, refs):
    bag = Bag()
    bag.scans = {"forward": Bag(), "backward": Bag()}
    for key, ref in zip(keys, refs):
        if isinstance(key, str):
            setattr(bag, key, ref)
        elif len(key) == 2:
            setattr(bag.scans[key[0]], key[1], ref)
        else:
            scan = bag.scans[key[0]]
            if not hasattr(scan, key[1]):
                setattr(scan, key[1], {})
            getattr(scan, key[1])[key[2]] = ref
    return bag


def shards(size, queries, keys, values, log_decay, gain, d_out):
    seq_size, dp_size, levels = size
    length, features = queries.shape[1:]
    heads = log_decay.shape[1]
    width = features // heads
    pairs = heads // 2
    steps = (seq_size.bit_length() - 1) + (dp_size.bit_length() - 1)
    spec = layout(length, pairs, width, levels, pairs >> levels, steps)
    names = list(spec)

    def body(*refs):
        kernel(size, width, refs[:6], refs[6:11], gathered(names, refs[11:]))

    whole = pl.BlockSpec(memory_space=pltpu.HBM)
    token = jax.ShapeDtypeStruct((length, features), BF16)
    flops = 2 * heads * length * width * (12 * length + 12 * width)
    results = (
        token, token, token,
        jax.ShapeDtypeStruct((heads, length), F32),
        jax.ShapeDtypeStruct((pairs, 2 * width), F32),
    )
    outputs = pl.pallas_call(
        body,
        out_shape=results,
        in_specs=[pl.BlockSpec(memory_space=pltpu.HBM)] * 6,
        out_specs=(whole,) * 5,
        scratch_shapes=list(spec.values()),
        compiler_params=pltpu.CompilerParams(
            collective_id=0, has_side_effects=True, vmem_limit_bytes=VMEM
        ),
        cost_estimate=pl.CostEstimate(
            flops=flops, bytes_accessed=14 * length * features, transcendentals=0
        ),
        name="gated_backward",
    )(queries[0], keys[0], values[0], log_decay[0], gain.reshape(pairs, 2 * width), d_out[0])
    d_queries, d_keys, d_values, d_log_decay, d_gain = pl.pallas_call(
        deliver,
        out_shape=results,
        in_specs=[pl.BlockSpec(memory_space=pl.ANY)] * 5,
        out_specs=(pl.BlockSpec(memory_space=pltpu.HBM),) * 5,
        scratch_shapes=[pltpu.VMEM(r.shape, r.dtype) for r in results]
        + [pltpu.SemaphoreType.DMA((5,))] * 2,
        compiler_params=pltpu.CompilerParams(vmem_limit_bytes=VMEM),
        cost_estimate=pl.CostEstimate(
            flops=0, bytes_accessed=12 * length * features, transcendentals=0
        ),
        name="deliver",
    )(*outputs)
    return d_queries[None], d_keys[None], d_values[None], d_log_decay[None], d_gain.reshape(-1)


def solution(mesh):
    seq_size, dp_size = mesh.shape["seq"], mesh.shape["dp"]
    levels = seq_size.bit_length() // 2
    tokens = P("dp", "seq", None)
    decays = P("dp", None, "seq")
    return jax.shard_map(
        functools.partial(shards, (seq_size, dp_size, levels)),
        mesh=mesh,
        in_specs=(tokens, tokens, tokens, decays, P(), tokens),
        out_specs=(tokens, tokens, tokens, decays, P()),
        check_vma=False,
    )
```

profile of v0, /device:TPU:1, one launch (start us, length us, event | category | flops | bytes accessed | tf_op | source)
XLA Modules:
  0.0 57.5 jit_solution(6021181263743611233)
XLA Ops:
  0.6 54.6 %gated_backward.1 = (bf16[128,2048]{1,0:T(8,128)(2,1)}, bf16[128,2048]{1,0:T(8,128)(2,1)}, bf16[128,2048]{1,0:T(8,128)(2,1)}, f32[32,128]{1,0:T(8,128)}, f32[16,128]{1,0:T(8,128)}) custom-call(bf16[128,2048]{1,0:T(8,128)(2,1)} %bitcast.11, bf16[128,2048]{1,0:T(8,128)(2,1)} %bitcast.12, bf16[128,2048]{1,0:T(8,128)(2,1)} %bitcast.13, f32[32,128]{1,0:T(8,128)} %bitcast.18, ...), custom_call_target="tpu_custom_call" | custom-call | flops 1207959552 | bytes 3670016 | tf_op jit(solution)/shard_map/gated_backward/pallas_call | solution.py:711
  55.3 2.3 %deliver.1 = (bf16[128,2048]{1,0:T(8,128)(2,1)}, bf16[128,2048]{1,0:T(8,128)(2,1)}, bf16[128,2048]{1,0:T(8,128)(2,1)}, f32[32,128]{1,0:T(8,128)}, f32[16,128]{1,0:T(8,128)}) custom-call(bf16[128,2048]{1,0:T(8,128)(2,1)} %get-tuple-element.15.refs_0_, bf16[128,2048]{1,0:T(8,128)(2,1)} %get-tuple-element.16.refs_1_, ...), custom_call_target="tpu_custom_call" | custom-call | bytes 3145728 | tf_op jit(solution)/shard_map/deliver/pallas_call | solution.py:725
where the time goes:
time: 57.8 us; the launch traced here: 57.5 us
  Pallas kernels  56.9 us (98%)
  between operations  0.64 us (1%)
    pallas_call x1, Pallas kernels, shards(): pl.pallas_call(body, out_shape=results, in_specs=[pl.BlockSpec(memory_spa...  54.6 us
    pallas_call x1, Pallas kernels, shards(): pl.pallas_call(deliver, out_shape=results, in_specs=[pl.BlockSpec(memory_...  2.27 us

commit v1 on v0

--- a/solution.py
+++ b/solution.py
@@ -297,10 +297,9 @@
         def _():
             x.chain_in[...] = jnp.zeros_like(x.chain_in)
 
-        begins = (place == start_place).astype(jnp.int32)
         for i in range(count):
             join(levels - 1, i)
-        works[levels](1 - begins)
+        works[levels]()
         for i in range(count):
             @pl.when(place != start_place)
             def _(i=i):
@@ -313,7 +312,7 @@
                 link(i).start()
 
             descend(levels - 1, i, x.chain_in[i])
-        works[levels + 1](begins)
+        works[levels + 1]()
         for level in range(levels - 1, 0, -1):
             order = range(halves[level])
             for i in order if level == levels - 1 else ordered(level):
@@ -358,24 +357,22 @@
             (s.query_t, pair, jnp.transpose(query)),
         ]
 
-    def cut(compute):
-        share = max(2, pairs // (2 * levels) // 2 * 2)
-        counts = [2] + [share] * (levels - 1)
-        left = pairs - sum(counts)
-        middle = left // 2 // 2 * 2
-        works, start = [], 0
+    def cut(compute, backward, per_hop):
+        distance = chain - 1 - place if backward else place
+        waits = (distance > 0).astype(jnp.int32)
+        ends = (distance == chain - 1).astype(jnp.int32)
+        counts = [2 * waits] + [2 + 2 * waits] * (levels - 1)
+        done = 0
+        works = []
         for count in counts:
-            works.append(functools.partial(each, start, count, compute))
-            start += count
-
-        def waiting(flag):
-            each(start, middle * flag, compute)
-
-        def closing(flag):
-            done = middle * (1 - flag)
-            each(start + done, left - done, compute)
-
-        return works + [waiting, closing]
+            works.append(functools.partial(each, done, count, compute))
+            done = done + count
+        left = pairs - done
+        middle = jnp.minimum(per_hop * distance, left)
+        middle = middle + ends * (left - middle)
+        works.append(functools.partial(each, done, middle, compute))
+        works.append(functools.partial(each, done + middle, left - middle, compute))
+        return works
 
     s.squares[...] = jnp.zeros_like(s.squares)
     s.products[...] = jnp.zeros_like(s.products)
@@ -415,7 +412,7 @@
     scan(
         "forward", s.fresh, s.start, False,
         lambda start, count: each(start, count, state_of, WIDE),
-        cut(inside), attend_after_loads,
+        cut(inside, False, 4), attend_after_loads,
     )
     features = pairs * pair_width
     mean = jnp.sum(s.squares[...], axis=1, keepdims=True) / features
@@ -483,13 +480,13 @@
     steps = len(partners)
 
     def with_gain(work, first, last):
-        def run(*flag):
-            work(*flag)
+        def run():
+            work()
             for step in range(first, last):
                 gain_advance(step)
         return run
 
-    works = cut(grads)
+    works = cut(grads, True, 2)
     begun = []
 
     def produce_slopes(start, count):

time: 57.8 us -> 55.2 us (0.955)
  Pallas kernels: 56.9 us -> 54.4 us
    pallas_call x1, Pallas kernels: 54.6 us -> 52.1 us  [shards(): pl.pallas_call(body, out_shape=results, in_specs=[pl.BlockSpec(memory_spa...]
where the time goes in v1:
time: 55.2 us; the launch traced here: 55 us
  Pallas kernels  54.4 us (99%)
  between operations  0.64 us (1%)
    pallas_call x1, Pallas kernels, shards(): pl.pallas_call(body, out_shape=results, in_specs=[pl.BlockSpec(memory_spa...  52.1 us
    pallas_call x1, Pallas kernels, shards(): pl.pallas_call(deliver, out_shape=results, in_specs=[pl.BlockSpec(memory_...  2.27 us

profile of v1, /device:TPU:1, one launch (start us, length us, event | category | flops | bytes accessed | tf_op | source)
XLA Modules:
  0.0 55.0 jit_solution(7473552995926897976)
XLA Ops:
  0.6 52.1 %gated_backward.1 = (bf16[128,2048]{1,0:T(8,128)(2,1)}, bf16[128,2048]{1,0:T(8,128)(2,1)}, bf16[128,2048]{1,0:T(8,128)(2,1)}, f32[32,128]{1,0:T(8,128)}, f32[16,128]{1,0:T(8,128)}) custom-call(bf16[128,2048]{1,0:T(8,128)(2,1)} %bitcast.11, bf16[128,2048]{1,0:T(8,128)(2,1)} %bitcast.12, bf16[128,2048]{1,0:T(8,128)(2,1)} %bitcast.13, f32[32,128]{1,0:T(8,128)} %bitcast.18, ...), custom_call_target="tpu_custom_call" | custom-call | flops 1207959552 | bytes 3670016 | tf_op jit(solution)/shard_map/gated_backward/pallas_call | solution.py:708
  52.7 2.3 %deliver.1 = (bf16[128,2048]{1,0:T(8,128)(2,1)}, bf16[128,2048]{1,0:T(8,128)(2,1)}, bf16[128,2048]{1,0:T(8,128)(2,1)}, f32[32,128]{1,0:T(8,128)}, f32[16,128]{1,0:T(8,128)}) custom-call(bf16[128,2048]{1,0:T(8,128)(2,1)} %get-tuple-element.15.refs_0_, bf16[128,2048]{1,0:T(8,128)(2,1)} %get-tuple-element.16.refs_1_, ...), custom_call_target="tpu_custom_call" | custom-call | bytes 3145728 | tf_op jit(solution)/shard_map/deliver/pallas_call | solution.py:722

commit v2 on v1

--- a/solution.py
+++ b/solution.py
@@ -13,7 +13,7 @@
 BF16 = jnp.bfloat16
 UNROLL = 2
 WIDE = 4
-VMEM = 58 * 1024 * 1024
+VMEM = 52 * 1024 * 1024
 
 
 def dot(a, b, contract, precision=None):
@@ -161,8 +161,6 @@
     s.late_rows[...] = jnp.exp(cum_rows[:, length - 1:length] - cum_rows)
     cum_columns = nt(causal.astype(F32), log_block, HIGH)
 
-    k_load.wait()
-    v_load.wait()
     for pair in range(pairs):
         first = jnp.broadcast_to(cum_columns[:, 2 * pair:2 * pair + 1], (length, length))
         second = jnp.broadcast_to(cum_columns[:, 2 * pair + 1:2 * pair + 2], (length, length))
@@ -170,9 +168,7 @@
         s.spread[2 * pair + 1] = second
         mixed = jnp.where(low_tok, first, second)
         total = mixed[length - 1:length, :]
-        s.grow[pair] = jnp.exp(mixed)
-        late = jnp.exp(total - mixed)
-        s.late[pair] = late
+        s.late[pair] = jnp.exp(total - mixed)
         s.decay[0, pair:pair + 1, :] = jnp.exp(total)
 
     def state_of(pair):
@@ -182,6 +178,8 @@
         fresh = packed(nn(lanes(key_t, key_t), rows(high, rest)))
         return [(s.key_t, pair, key_t), (s.fresh, pair, fresh)]
 
+    k_load.wait()
+    v_load.wait()
     pl.semaphore_wait(barrier, len(greeted))
 
     bits = [bit_of(me, level) for level in range(levels)]
@@ -243,17 +241,26 @@
                 x.first[level][offset + i] = earlier
                 x.total[level][offset + i] = later_decay * earlier + later
 
-        produce(gives[0], halves[0])
-        start_up(0)
-        produce(keeps[0], halves[0])
+        for index, (offset, size) in enumerate(pieces(0)):
+            produce(gives[0] + offset, size)
+            if index == 0 and not backward:
+                decay_copy(0).start()
+            up(0, index).start()
+        offset, size = pieces(0)[0]
+        produce(keeps[0] + offset, size)
         for level in range(levels):
-            works[level]()
+            if level > 0:
+                works[level]()
             if not backward:
                 decay_copy(level).wait()
                 s.decay[level + 1] = s.decay[level] * s.decay_other[level]
             if level < levels - 1:
                 join(level, 0)
                 start_up(level + 1)
+                if level == 0:
+                    offset, size = pieces(0)[1]
+                    produce(keeps[0] + offset, size)
+                    works[0]()
                 join(level, 1)
 
         start_place = chain - 1 if backward else 0
@@ -342,6 +349,7 @@
 
     def inside(pair):
         query = q_ref[:, columns(pair)]
+        grow = jnp.exp(jnp.where(low_tok, s.spread[2 * pair], s.spread[2 * pair + 1]))
         scores = nt(query, stacked(k_ref[:, columns(pair)]))
         tables = []
         for head in range(2):
@@ -354,7 +362,7 @@
         return [
             (s.table, pair, table), (s.score_high, pair, high),
             (s.score_rest, pair, rest), (s.attended, pair, part),
-            (s.query_t, pair, jnp.transpose(query)),
+            (s.query_t, pair, jnp.transpose(query)), (s.grow, pair, grow),
         ]
 
     def cut(compute, backward, per_hop):
@@ -492,10 +500,10 @@
     def produce_slopes(start, count):
         each(start, count, slopes, WIDE)
         begun.append(True)
-        if len(begun) == 2:
+        if len(begun) == 4:
             gain_step(0).start()
 
-    spread_steps = [steps * i // (levels + 2) for i in range(levels + 3)]
+    spread_steps = [0] + [steps * i // (levels + 1) for i in range(levels + 2)]
     works = [
         with_gain(work, spread_steps[i], spread_steps[i + 1]) for i, work in enumerate(works)
     ]
@@ -571,21 +579,14 @@
 
 
 def deliver(*refs):
-    sources, targets, held, (read, wrote) = refs[:5], refs[5:10], refs[10:15], refs[15:]
-    reads = [
-        pltpu.make_async_copy(source, place, read.at[index])
-        for index, (source, place) in enumerate(zip(sources, held))
+    sources, targets, done = refs[:5], refs[5:10], refs[10]
+    copies = [
+        pltpu.make_async_copy(source, target, done.at[index])
+        for index, (source, target) in enumerate(zip(sources, targets))
     ]
-    writes = [
-        pltpu.make_async_copy(place, target, wrote.at[index])
-        for index, (place, target) in enumerate(zip(held, targets))
-    ]
-    for copy in reads:
+    for copy in copies:
         copy.start()
-    for copy, following in zip(reads, writes):
-        copy.wait()
-        following.start()
-    for copy in writes:
+    for copy in copies:
         copy.wait()
 
 
@@ -697,7 +698,7 @@
     def body(*refs):
         kernel(size, width, refs[:6], refs[6:11], gathered(names, refs[11:]))
 
-    whole = pl.BlockSpec(memory_space=pltpu.HBM)
+    whole = pl.BlockSpec(memory_space=pl.ANY)
     token = jax.ShapeDtypeStruct((length, features), BF16)
     flops = 2 * heads * length * width * (12 * length + 12 * width)
     results = (
@@ -724,9 +725,7 @@
         out_shape=results,
         in_specs=[pl.BlockSpec(memory_space=pl.ANY)] * 5,
         out_specs=(pl.BlockSpec(memory_space=pltpu.HBM),) * 5,
-        scratch_shapes=[pltpu.VMEM(r.shape, r.dtype) for r in results]
-        + [pltpu.SemaphoreType.DMA((5,))] * 2,
-        compiler_params=pltpu.CompilerParams(vmem_limit_bytes=VMEM),
+        scratch_shapes=[pltpu.SemaphoreType.DMA((5,))],
         cost_estimate=pl.CostEstimate(
             flops=0, bytes_accessed=12 * length * features, transcendentals=0
         ),

time: 55.2 us -> 106 us (1.92)
  Pallas kernels: 54.4 us -> 100 us
  local copies, waits for them, and re-layouts: 0 us -> 5 us
    pallas_call x1, Pallas kernels: 2.27 us -> 49.5 us  [shards(): pl.pallas_call(deliver, out_shape=results, in_specs=[pl.BlockSpec(memory_...]
    unnamed x0 -> x14, local copies, waits for them, and re-layouts: none -> 5 us
    pallas_call x1, Pallas kernels: 52.1 us -> 50.9 us  [shards(): pl.pallas_call(body, out_shape=results, in_specs=[pl.BlockSpec(memory_spa...]
where the time goes in v2:
time: 106 us
  Pallas kernels  100 us (94%)
  local copies, waits for them, and re-layouts  5 us (5%)
    pallas_call x1, Pallas kernels, shards(): pl.pallas_call(body, out_shape=results, in_specs=[pl.BlockSpec(memory_spa...  50.9 us
    pallas_call x1, Pallas kernels, shards(): pl.pallas_call(deliver, out_shape=results, in_specs=[pl.BlockSpec(memory_...  49.5 us
    unnamed x14, local copies, waits for them, and re-layouts  5 us

profile of v2, /device:TPU:1, one launch (start us, length us, event | category | flops | bytes accessed | tf_op | source)
XLA Modules:
  0.0 106.1 jit_solution(12727281563585155855)
XLA Ops:
  0.6 0.0 copy-start.6
  0.6 0.7 copy-done.6
  1.3 0.0 copy-start.5
  1.3 0.7 copy-done.5
  2.0 50.9 %gated_backward.1 = (bf16[128,2048]{1,0:T(8,128)(2,1)S(1)}, bf16[128,2048]{1,0:T(8,128)(2,1)S(1)}, bf16[128,2048]{1,0:T(8,128)(2,1)S(1)}, f32[32,128]{1,0:T(8,128)S(1)}, f32[16,128]{1,0:T(8,128)S(1)}) custom-call(bf16[128,2048]{1,0:T(8,128)(2,1)} %bitcast.13, bf16[128,2048]{1,0:T(8,128)(2,1)} %bitcast.14, bf16[128,2048]{1,0:T(8,128)(2,1)} %bitcast.15, ...), custom_call_target="tpu_custom_call" | custom-call | flops 1207959552 | bytes 3670016 | tf_op jit(solution)/shard_map/gated_backward/pallas_call | solution.py:709
  53.0 0.0 copy-start
  53.0 0.8 copy-done
  53.8 0.0 copy-start.1
  53.8 0.8 copy-done.1
  54.6 0.0 copy-start.2
  54.6 0.8 copy-done.2
  55.4 0.0 copy-start.3
  55.4 0.6 copy-done.3
  56.0 0.0 copy-start.4
  56.0 0.6 copy-done.4
  56.6 49.5 %deliver.1 = (bf16[128,2048]{1,0:T(8,128)(2,1)}, bf16[128,2048]{1,0:T(8,128)(2,1)}, bf16[128,2048]{1,0:T(8,128)(2,1)}, f32[32,128]{1,0:T(8,128)}, f32[16,128]{1,0:T(8,128)}) custom-call(bf16[128,2048]{1,0:T(8,128)(2,1)} %copy-done, bf16[128,2048]{1,0:T(8,128)(2,1)} %copy-done.1, bf16[128,2048]{1,0:T(8,128)(2,1)} %copy-done.2, f32[32,128]{1,0:T(8,128)} %copy-done.3, ...), custom_call_target="tpu_custom_call" | custom-call | bytes 3145728 | tf_op jit(solution)/shard_map/deliver/pallas_call | solution.py:723
Async XLA Ops:
  0.6 0.7 copy-start.6
  1.3 0.7 copy-start.5
  53.0 0.8 copy-start
  53.8 0.8 copy-start.1
  54.6 0.8 copy-start.2
  55.4 0.6 copy-start.3
  56.0 0.6 copy-start.4
